TPU v7x, 32 devices: a whole 2x2x4 slice. The times are simulated.
32 devices in a mesh: dom: 2 (over x), space: 16 (over z, y, core).
Axes of the slice: x: 2, y: 2, z: 4, core: 2. Of those that a mesh axis runs over, the one named last changes fastest.
Arguments:
- inputs: bfloat16 [2, 32, 2048, 2048], P('dom', None, 'space'), parts along dimension 0, may hold values from -10.5 to 10.5
- target: bfloat16 [2, 32, 2048, 2048], P('dom', None, 'space'), parts along dimension 0, may hold values from -6 to 6
- spectral_weight: float32 [64, 32, 32, 128], P('space'), may hold values from -18 to 18
- local_weight: bfloat16 [32, 32], replicated, may hold values from -1 to 1
- bias_term: float32 [32], replicated, may hold values from -3 to 3
Outputs:
- grad_input: bfloat16 [2, 32, 2048, 2048], P('dom', None, 'space'), parts along dimension 0
- grad_spectral: float32 [64, 64, 32, 128], P('space', 'dom'), parts along dimension 1
- grad_local: float32 [64, 32], P('dom'), parts along dimension 0
- grad_bias: float32 [64], P('dom'), parts along dimension 0
There are 2 independent parts, one for each index of `dom`. A program takes and returns all parts, laid end to end along the dimension named above; an argument that names none is the same for every part. Nothing has to cross between parts.
All inputs are finite; a program needn't handle non-finite values.
Results may differ from a plain program's by a relative error of at most 0.014.
Values may be sent and summed in bfloat16 or wider, within the bound.
A program may use at most 192 MiB of HBM per device.

v0:
```python
import math
import jax
import jax.numpy as jnp
from jax import lax
from jax.sharding import PartitionSpec as P

H = 2048
W = 2048
KX = 64
KY = 64
PRECISE = lax.Precision.HIGHEST


def row_table():
    mode_index = jnp.arange(KY, dtype=jnp.int32)[:, None]
    column = jnp.arange(W, dtype=jnp.int32)[None, :]
    angles = (mode_index * column % W).astype(jnp.float32) * (2.0 * math.pi / W)
    factor = 1.0 / math.sqrt(H * W)
    return jnp.stack([jnp.cos(angles) * factor, -jnp.sin(angles) * factor]).astype(jnp.bfloat16)


def column_table(row_index):
    column = jnp.arange(KX, dtype=jnp.int32)
    frequency = jnp.where(column < KX // 2, column, column + H - KX)
    angles = (row_index[:, None] * frequency[None, :] % H).astype(jnp.float32) * (2.0 * math.pi / H)
    return jnp.concatenate([jnp.cos(angles), jnp.sin(angles)], axis=1)


def mode_weights(start_mode, mode_count):
    mode_index = start_mode + jnp.arange(mode_count, dtype=jnp.int32)
    return jnp.where(mode_index == 0, 1.0, 2.0).astype(jnp.float32)


def row_analysis(field_data, basis):
    return jnp.einsum("schw,pkw->kpsch", field_data, basis, preferred_element_type=jnp.float32)


def row_synth(spectra, basis):
    return jnp.einsum("kpsch,pkw->schw", spectra, basis, preferred_element_type=jnp.float32)


def column_modes(slab_part, basis):
    product = jnp.einsum("kpsch,hj->kpscj", slab_part, basis, precision=PRECISE)
    half_count = basis.shape[1] // 2
    real_part = product[:, 0, :, :, :half_count] + product[:, 1, :, :, half_count:]
    imag_part = product[:, 1, :, :, :half_count] - product[:, 0, :, :, half_count:]
    return jnp.concatenate([real_part, imag_part], axis=-1)


def column_synth(mode_data, basis):
    half_count = basis.shape[1] // 2
    real_part, imag_part = (mode_data[..., :half_count], mode_data[..., half_count:])
    cosines, sine_part = (basis[:, :half_count], basis[:, half_count:])
    first_part = jnp.einsum("ysok,hk->ysoh", real_part, cosines, precision=PRECISE) - jnp.einsum(
        "ysok,hk->ysoh", imag_part, sine_part, precision=PRECISE
    )
    second = jnp.einsum("ysok,hk->ysoh", real_part, sine_part, precision=PRECISE) + jnp.einsum(
        "ysok,hk->ysoh", imag_part, cosines, precision=PRECISE
    )
    return jnp.stack([first_part, second], axis=1).astype(jnp.bfloat16)


def split_complex(mode_data):
    half_count = mode_data.shape[-1] // 2
    return (mode_data[..., :half_count], mode_data[..., half_count:])


def mix_modes(input_modes, weight):
    spec_real, spec_imag = split_complex(input_modes)
    weight_real, weight_imag = split_complex(weight)
    form = "ysck,ycok->ysok"
    out_real = jnp.einsum(form, spec_real, weight_real, precision=PRECISE) - jnp.einsum(
        form, spec_imag, weight_imag, precision=PRECISE
    )
    out_imag = jnp.einsum(form, spec_real, weight_imag, precision=PRECISE) + jnp.einsum(
        form, spec_imag, weight_real, precision=PRECISE
    )
    return jnp.concatenate([out_real, out_imag], axis=-1)


def mix_back(delta_modes, weight):
    delta_real, delta_imag = split_complex(delta_modes)
    weight_real, weight_imag = split_complex(weight)
    form = "ysok,ycok->ysck"
    out_real = jnp.einsum(form, delta_real, weight_real, precision=PRECISE) + jnp.einsum(
        form, delta_imag, weight_imag, precision=PRECISE
    )
    out_imag = jnp.einsum(form, delta_imag, weight_real, precision=PRECISE) - jnp.einsum(
        form, delta_real, weight_imag, precision=PRECISE
    )
    return jnp.concatenate([out_real, out_imag], axis=-1)


def mix_grad(input_modes, delta_modes):
    spec_real, spec_imag = split_complex(input_modes)
    delta_real, delta_imag = split_complex(delta_modes)
    form = "ysck,ysok->ycok"
    grad_real = jnp.einsum(form, spec_real, delta_real, precision=PRECISE) + jnp.einsum(
        form, spec_imag, delta_imag, precision=PRECISE
    )
    grad_imag = jnp.einsum(form, spec_real, delta_imag, precision=PRECISE) - jnp.einsum(
        form, spec_imag, delta_real, precision=PRECISE
    )
    return jnp.concatenate([grad_real, grad_imag], axis=-1)


def gelu_parts(value):
    normal_cdf = 0.5 * (1.0 + jax.scipy.special.erf(value * (1.0 / math.sqrt(2.0))))
    density = jnp.exp(-0.5 * value * value) * (1.0 / math.sqrt(2.0 * math.pi))
    return (value * normal_cdf, normal_cdf + value * density)


def per_device(inputs, target, spectral_weight, local_weight, bias_term):
    mode_block = spectral_weight.shape[0]
    row_count = inputs.shape[2]
    device = lax.axis_index("space")
    row_basis = row_table()
    column_basis = column_table(jnp.arange(H, dtype=jnp.int32))
    own_basis = column_table(device * row_count + jnp.arange(row_count, dtype=jnp.int32))
    mode_gain = mode_weights(device * mode_block, mode_block)[:, None, None, None]

    def to_modes(field_data):
        row_modes = row_analysis(field_data, row_basis)
        return lax.psum_scatter(
            column_modes(row_modes, own_basis), "space", scatter_dimension=0, tiled=True
        )

    def to_rows(mode_data):
        column_part = column_synth(mode_data, column_basis)
        return row_synth(
            lax.all_to_all(column_part, "space", split_axis=4, concat_axis=0, tiled=True), row_basis
        )

    input_modes = to_modes(inputs)
    mixed_modes = mix_modes(input_modes, spectral_weight) * mode_gain
    local_term = jnp.einsum(
        "co,schw->sohw", local_weight, inputs, preferred_element_type=jnp.float32
    )
    preact = to_rows(mixed_modes) + local_term + bias_term[None, :, None, None]
    activated, derivative = gelu_parts(preact)
    delta_pre = ((activated - target.astype(jnp.float32)) * derivative).astype(jnp.bfloat16)
    delta_modes = to_modes(delta_pre) * mode_gain
    grad_spectral = mix_grad(input_modes, delta_modes)
    back_modes = mix_back(delta_modes, spectral_weight)
    back_local = jnp.einsum(
        "co,sohw->schw", local_weight, delta_pre, preferred_element_type=jnp.float32
    )
    grad_input = (to_rows(back_modes) + back_local).astype(jnp.bfloat16)
    weight_term = jnp.einsum("schw,sohw->co", inputs, delta_pre, preferred_element_type=jnp.float32)
    bias_sum = jnp.sum(delta_pre, axis=(0, 2, 3), dtype=jnp.float32)
    weight_total, bias_total = lax.psum((weight_term, bias_sum), "space")
    cell_count = inputs.shape[0] * H * W
    return (grad_input, grad_spectral, weight_total / cell_count, bias_total / cell_count)


def solution(mesh):
    return jax.shard_map(
        per_device,
        mesh=mesh,
        in_specs=(
            P("dom", None, "space", None),
            P("dom", None, "space", None),
            P("space", None, None, None),
            P(),
            P(),
        ),
        out_specs=(
            P("dom", None, "space", None),
            P("space", "dom", None, None),
            P("dom", None),
            P("dom"),
        ),
        check_vma=False,
    )
```

profile of v0, /device:TPU:0, one launch (start us, length us, event | category | flops | bytes accessed | tf_op | source)
XLA Modules:
  0.0 490.5 jit_solution(4571138129678116677)
XLA Ops:
  7.2 0.0 copy-start
  7.2 0.0 reduce-scatter.3.cloned.1.call-start
  7.2 2.2 multiply_convert_fusion
  9.4 0.3 fusion.101
  9.8 0.0 copy-start.1
  9.8 10.8 %fusion.37 = f32[64,2,32,128]{3,0,2,1:T(8,128)} fusion(bf16[1,32,128,2048]{3,2,1,0:T(8,128)(2,1)} %param.5, bf16[1,64,2048]{2,1,0:T(8,128)(2,1)S(1)} %get-tuple-element.42, bf16[1,64,2048]{2,1,0:T(8,128)(2,1)S(1)} %get-tuple-element.43), kind=kOutput, calls=%fused_computation.52 | convolution fusion | flops 2148532224 | bytes 19398656 | tf_op jit(solution)/shard_map/schw,pkw->kpsch/dot_general | solution.py:35
  20.6 4.9 fusion.31
  25.5 0.3 fusion.50
  25.8 0.3 fusion.52
  26.2 1.3 pad_maximum_fusion.1
  27.5 0.0 reduce-scatter.3.cloned.1.call-update
  27.5 60.3 %reduce-scatter.3.cloned.1.call-done = f32[4,1,32,128]{3,2,0,1:T(8,128)} async-done(((f32[64,1,32,128]{3,2,0,1:T(8,128)}), f32[4,1,32,128]{3,2,0,1:T(8,128)}) %reduce-scatter.3.cloned.1.call-update) | async-done | bytes 65552 | tf_op jit(solution)/shard_map/reduce_scatter | solution.py:124
  87.8 1.0 slice_bitcast_fusion.7
  88.8 0.0 copy-done.1
  88.8 1.0 multiply_reduce_fusion.6
  89.9 0.1 maximum_multiply_fusion
  90.0 2.9 fusion.62
  92.9 2.9 fusion.69
  95.8 3.6 fusion.25
  99.4 3.2 fusion.26
  102.7 1.1 pad_maximum_fusion.2
  103.7 6.8 %copy.27 = bf16[4,2,1,32,2048]{3,0,2,1,4:T(4,128)(2,1)} copy(bf16[4,2,1,32,2048]{4,3,0,2,1:T(8,128)(2,1)} %pad_maximum_fusion.2) | data formatting | bytes 2097152 | tf_op jit(solution)/shard_map/stack | solution.py:60
  110.5 7.7 %reshape.437 = bf16[16,2,16384]{2,1,0:T(2,128)(2,1)} reshape(bf16[2048,2,1,4,32]{4,3,2,1,0:T(4,128)(2,1)} %bitcast.233) | data formatting | bytes 2097152
  118.2 4.3 all-to-all-start
  122.5 0.0 reduce-scatter.5.cloned.1.call-start
  122.6 0.0 copy-done
  122.6 0.0 copy-start.3
  122.6 22.5 %fusion.17 = f32[128,2048,32]{1,2,0:T(8,128)} fusion(bf16[32,128,2048]{2,1,0:T(8,128)(2,1)} %bitcast.229, bf16[32,32]{1,0:T(8,128)(2,1)S(1)} %copy-done), kind=kOutput, calls=%fused_computation.21 | convolution fusion | flops 536870912 | bytes 50333696 | tf_op jit(solution)/shard_map/co,schw->sohw/dot_general | solution.py:136
  145.1 0.3 all-to-all-done
  145.5 7.3 %reshape.438 = bf16[2048,2,1,4,32]{4,3,2,1,0:T(4,128)(2,1)} reshape(bf16[16,2,16384]{2,1,0:T(2,128)(2,1)} %all-to-all-done) | data formatting | bytes 2097152
  152.8 7.1 %copy.28 = bf16[4,2,1,32,16,128]{5,0,4,1,3,2:T(4,128)(2,1)} copy(bf16[4,2,1,32,16,128]{3,0,1,5,4,2:T(4,128)(2,1)} %bitcast.234) | data formatting | bytes 2097152 | tf_op jit(solution)/shard_map/all_to_all | solution.py:131
  159.9 0.0 copy-done.3
  159.9 38.7 %convert_reduce_fusion = (f32[32]{0:T(128)S(1)}, bf16[1,32,128,2048]{3,2,1,0:T(8,128)(2,1)}) fusion(bf16[1,32,128,2048]{3,2,1,0:T(8,128)(2,1)} %param.6, f32[32]{0:T(128)S(1)} %copy-done.3, f32[128,2048,32]{1,2,0:T(8,128)} %fusion.17, bf16[64,2,32,128]{3,0,1,2:T(8,128)(2,1)} %bitcast.238, bf16[1,64,2048]{2,1,0:T(8,128)(2,1)S(1)} %get-tuple-element.42, ...), kind=kOutput, calls=%fused_computation.11 | convolution fusion | flops 2290352128 | bytes 68681984 | tf_op jit(solution)/shard_map/kpsch,pkw->schw/dot_general | solution.py:39
  198.6 10.5 %fusion.40 = f32[64,2,32,128]{3,0,2,1:T(8,128)} fusion(bf16[1,32,128,2048]{3,2,1,0:T(8,128)(2,1)} %get-tuple-element.41, bf16[1,64,2048]{2,1,0:T(8,128)(2,1)S(1)} %get-tuple-element.42, bf16[1,64,2048]{2,1,0:T(8,128)(2,1)S(1)} %get-tuple-element.43), kind=kOutput, calls=%fused_computation.53 | convolution fusion | flops 2148532224 | bytes 19398656 | tf_op jit(solution)/shard_map/schw,pkw->kpsch/dot_general | solution.py:35
  209.1 4.6 fusion.34
  213.7 0.6 fusion.49
  214.3 1.3 pad_maximum_fusion.3
  215.6 0.0 reduce-scatter.5.cloned.1.call-update
  215.7 84.2 %fusion.43 = f32[32,32]{0,1:T(8,128)S(1)} fusion(bf16[32,128,2048]{2,1,0:T(8,128)(2,1)} %bitcast.230, bf16[32,128,2048]{2,1,0:T(8,128)(2,1)} %bitcast.231), kind=kOutput, calls=%fused_computation.54 | convolution fusion | flops 536870912 | bytes 33558528 | tf_op jit(solution)/shard_map/schw,sohw->co/dot_general | solution.py:149
  299.9 62.8 %all-reduce = (f32[32,32]{0,1:T(8,128)S(1)}, f32[32]{0:T(128)S(1)}) all-reduce(f32[32,32]{0,1:T(8,128)S(1)} %fusion.43, f32[32]{0:T(128)S(1)} %get-tuple-element.40), channel_id=1, replica_groups=mesh['dom'=2,'space'=16] {'space'}, use_global_device_ids=true, to_apply=%region_2.3 | all-reduce | flops 1056 | bytes 8448 | tf_op jit(solution)/shard_map/psum | solution.py:151
  362.7 0.0 reduce-scatter.5.cloned.1.call-done
  362.7 0.9 broadcast_multiply_fusion
  363.6 0.1 slice_bitcast_fusion.2
  363.7 4.3 add_bitcast_fusion
  368.0 2.9 fusion.59
  370.9 2.9 fusion.66
  373.8 3.2 fusion.23
  377.0 3.2 fusion.24
  380.3 0.1 pad_maximum_fusion.4
  380.4 5.0 %copy.34 = bf16[4,2,1,32,2048]{3,0,2,1,4:T(4,128)(2,1)} copy(bf16[4,2,1,32,2048]{4,3,0,2,1:T(8,128)(2,1)S(1)} %pad_maximum_fusion.4) | data formatting | bytes 2097152 | tf_op jit(solution)/shard_map/stack | solution.py:60
  385.4 7.6 %reshape.439 = bf16[16,2,16384]{2,1,0:T(2,128)(2,1)} reshape(bf16[2048,2,1,4,32]{4,3,2,1,0:T(4,128)(2,1)} %bitcast.235) | data formatting | bytes 2097152
  393.0 4.3 all-to-all-start.1
  397.4 0.7 copy.40
  398.0 0.5 broadcast_multiply_fusion.2
  398.6 0.0 copy-start.2
  398.6 35.7 %fusion.14 = f32[128,2048,32]{1,2,0:T(8,128)} fusion(bf16[32,128,2048]{2,1,0:T(8,128)(2,1)} %bitcast.232, bf16[32,32]{1,0:T(8,128)(2,1)S(1)} %copy-done), kind=kOutput, calls=%fused_computation.18 | convolution fusion | flops 536870912 | bytes 50333696 | tf_op jit(solution)/shard_map/co,sohw->schw/dot_general | solution.py:145
  434.2 0.0 copy-done.2
  434.2 3.6 pad_maximum_fusion
  437.8 0.0 all-to-all-done.1
  437.8 7.3 %reshape.440 = bf16[2048,2,1,4,32]{4,3,2,1,0:T(4,128)(2,1)} reshape(bf16[16,2,16384]{2,1,0:T(2,128)(2,1)} %all-to-all-done.1) | data formatting | bytes 2097152
  445.2 6.1 %copy.35 = bf16[4,2,1,32,16,128]{5,0,4,1,3,2:T(4,128)(2,1)S(1)} copy(bf16[4,2,1,32,16,128]{3,0,1,5,4,2:T(4,128)(2,1)} %bitcast.236) | data formatting | bytes 2097152 | tf_op jit(solution)/shard_map/all_to_all | solution.py:131
  451.3 31.9 %fusion.6 = bf16[1,32,128,2048]{3,2,1,0:T(8,128)(2,1)} fusion(f32[128,2048,32]{1,2,0:T(8,128)} %fusion.14, bf16[64,2,32,128]{3,0,1,2:T(8,128)(2,1)S(1)} %bitcast.237, bf16[1,64,2048]{2,1,0:T(8,128)(2,1)S(1)} %get-tuple-element.42, bf16[1,64,2048]{2,1,0:T(8,128)(2,1)S(1)} %get-tuple-element.43), kind=kOutput, calls=%fused_computation.8 | convolution fusion | flops 2164523008 | bytes 51904512 | tf_op jit(solution)/shard_map/kpsch,pkw->schw/dot_general | solution.py:39
  (6 shorter events, 0.0 us)
Async XLA Ops:
  7.2 115.4 %copy-start = (bf16[32,32]{1,0:T(8,128)(2,1)S(1)}, bf16[32,32]{1,0:T(8,128)(2,1)}, u32[]{:S(2)}) copy-start(bf16[32,32]{1,0:T(8,128)(2,1)} %param.8) | copy-start | bytes 6148
  7.2 80.6 %reduce-scatter.3.cloned.1.call-start = ((), (), s32[]{:S(2)}) async-start(), calls=%async_computation.4 | async-start | bytes 1114112 | tf_op jit(solution)/shard_map/reduce_scatter | solution.py:124
  9.8 79.0 %copy-start.1 = (f32[4,32,32,128]{3,2,1,0:T(8,128)S(1)}, f32[4,32,32,128]{3,2,1,0:T(8,128)}, u32[]{:S(2)}) copy-start(f32[4,32,32,128]{3,2,1,0:T(8,128)} %param.7) | copy-start | bytes 6291460
  118.2 27.3 %all-to-all-start = ((bf16[16,2,16384]{2,1,0:T(2,128)(2,1)}), bf16[16,2,16384]{2,1,0:T(2,128)(2,1)}, u32[]{:S(2)}, u32[]{:S(2)}) async-start(bf16[16,2,16384]{2,1,0:T(2,128)(2,1)} %reshape.437), calls=%async_computation.1 | async-start | bytes 2097152 | tf_op jit(solution)/shard_map/all_to_all | solution.py:131
  122.5 240.1 %reduce-scatter.5.cloned.1.call-start = ((), (), s32[]{:S(2)}) async-start(), calls=%async_computation.5 | async-start | bytes 1114112 | tf_op jit(solution)/shard_map/reduce_scatter | solution.py:124
  122.6 37.3 %copy-start.3 = (f32[32]{0:T(128)S(1)}, f32[32]{0:T(128)}, u32[]{:S(2)}) copy-start(f32[32]{0:T(128)} %param.9) | copy-start | bytes 388
  393.0 44.8 %all-to-all-start.1 = ((bf16[16,2,16384]{2,1,0:T(2,128)(2,1)}), bf16[16,2,16384]{2,1,0:T(2,128)(2,1)}, u32[]{:S(2)}, u32[]{:S(2)}) async-start(bf16[16,2,16384]{2,1,0:T(2,128)(2,1)} %reshape.439), calls=%async_computation.3 | async-start | bytes 2097152 | tf_op jit(solution)/shard_map/all_to_all | solution.py:131
  398.6 35.7 %copy-start.2 = (f32[4,32,32,64]{3,2,1,0:T(8,128)S(1)}, f32[4,32,32,64]{3,2,1,0:T(8,128)}, u32[]{:S(2)}) copy-start(f32[4,32,32,64]{3,2,1,0:T(8,128)} %get-tuple-element.28) | copy-start | bytes 3145732
Sparse Core Ops, SparseCore 0:
  27.6 60.1 reduce-scatter.2
  215.8 59.5 reduce-scatter.4
where the time goes:
time: 495 us; the launch traced here: 490 us
  matrix products  269 us (54%)
  blocking collectives  62.8 us (13%)
  waiting for transfers between devices  60.6 us (12%)
  local copies, waits for them, and re-layouts  56.8 us (11%)
  other arithmetic  18 us (4%)
  between operations  14.8 us (3%)
  starting transfers between devices  8.74 us (2%)
    dot_general x1, matrix products, per_device(): jnp.einsum('schw,sohw->co', inputs, delta_pre, preferred_element_type=jnp...  84.2 us
    dot_general x2, matrix products, row_synth(): jnp.einsum('kpsch,pkw->schw', spectra, basis, preferred_element_type=jnp....  70.6 us
    psum x1, blocking collectives, per_device(): weight_total, bias_total = lax.psum((weight_term, bias_sum), 'space')  62.8 us
    reduce_scatter x2, waiting for transfers between devices, to_modes(): lax.psum_scatter(column_modes(row_modes, own_basis), 'space', scatter_dim...  60.3 us
    dot_general x1, matrix products, per_device(): jnp.einsum('co,sohw->schw', local_weight, delta_pre, preferred_element_ty...  35.7 us
    unnamed x15, local copies, waits for them, and re-layouts  31.8 us
    dot_general x1, matrix products, per_device(): jnp.einsum('co,schw->sohw', local_weight, inputs, preferred_element_type=...  22.5 us
    dot_general x2, matrix products, row_analysis(): jnp.einsum('schw,pkw->kpsch', field_data, basis, preferred_element_type=j...  21.3 us
  transfers between devices with their start and end apart: 4, of which 2 were waited for; matrix products, arithmetic and copies ran while one was open for 30% of the time, Pallas kernels for 0%

commit v1 on v0

--- a/solution.py
+++ b/solution.py
@@ -128,7 +128,13 @@
     def to_rows(mode_data):
         column_part = column_synth(mode_data, column_basis)
         return row_synth(
-            lax.all_to_all(column_part, "space", split_axis=4, concat_axis=0, tiled=True), row_basis
+            jnp.concatenate(
+                lax.all_to_all(
+                    jnp.stack(jnp.split(column_part, lax.axis_size("space"), axis=4)), "space", 0, 0
+                ),
+                axis=0,
+            ),
+            row_basis,
         )
 
     input_modes = to_modes(inputs)

time: 495 us -> 464 us (0.937)
  local copies, waits for them, and re-layouts: 56.8 us -> 23.7 us
    another operation x2 -> x0, local copies, waits for them, and re-layouts: 11.8 us -> none  [column_synth(): return jnp.stack([first_part, second], axis=1).astype(jnp.bfloat16)]
    unnamed x15 -> x41, local copies, waits for them, and re-layouts: 31.8 us -> 21 us
    all_to_all x2, local copies, waits for them, and re-layouts: 13.2 us -> 2.7 us  [to_rows(): lax.all_to_all(jnp.stack(jnp.split(column_part, lax.axis_size('space'), a...]
    dot_general x2, matrix products: 70.6 us -> 79 us  [row_synth(): jnp.einsum('kpsch,pkw->schw', spectra, basis, preferred_element_type=jnp....]
    dot_general x1, matrix products: 84.2 us -> 78 us  [per_device(): jnp.einsum('schw,sohw->co', inputs, delta_pre, preferred_element_type=jnp...]
  transfers between devices with their start and end apart: 4 -> 4, of which waited for: 2 -> 2; matrix products, arithmetic and copies ran while one was open for 30% -> 31% of each run, Pallas kernels for 0% -> 0%
where the time goes in v1:
time: 464 us; the launch traced here: 461 us
  matrix products  271 us (58%)
  blocking collectives  62.9 us (14%)
  waiting for transfers between devices  60.6 us (13%)
  local copies, waits for them, and re-layouts  23.7 us (5%)
  other arithmetic  18.3 us (4%)
  between operations  14.8 us (3%)
  starting transfers between devices  8.74 us (2%)
    dot_general x2, matrix products, row_synth(): jnp.einsum('kpsch,pkw->schw', spectra, basis, preferred_element_type=jnp....  79 us
    dot_general x1, matrix products, per_device(): jnp.einsum('schw,sohw->co', inputs, delta_pre, preferred_element_type=jnp...  78 us
    psum x1, blocking collectives, per_device(): weight_total, bias_total = lax.psum((weight_term, bias_sum), 'space')  62.9 us
    reduce_scatter x2, waiting for transfers between devices, to_modes(): lax.psum_scatter(column_modes(row_modes, own_basis), 'space', scatter_dim...  60.3 us
    dot_general x1, matrix products, per_device(): jnp.einsum('co,sohw->schw', local_weight, delta_pre, preferred_element_ty...  35.8 us
    dot_general x1, matrix products, per_device(): jnp.einsum('co,schw->sohw', local_weight, inputs, preferred_element_type=...  22.5 us
    dot_general x2, matrix products, row_analysis(): jnp.einsum('schw,pkw->kpsch', field_data, basis, preferred_element_type=j...  21.8 us
    unnamed x41, local copies, waits for them, and re-layouts  21 us
  transfers between devices with their start and end apart: 4, of which 2 were waited for; matrix products, arithmetic and copies ran while one was open for 31% of the time, Pallas kernels for 0%

profile of v1, /device:TPU:0, one launch (start us, length us, event | category | flops | bytes accessed | tf_op | source)
XLA Modules:
  0.0 460.6 jit_solution(14848506588378217110)
XLA Ops:
  7.2 2.2 multiply_convert_fusion
  9.8 10.8 %fusion.37 = f32[64,2,32,128]{3,0,2,1:T(8,128)} fusion(bf16[1,32,128,2048]{3,2,1,0:T(8,128)(2,1)} %param.5, bf16[1,64,2048]{2,1,0:T(8,128)(2,1)S(1)} %get-tuple-element.42, bf16[1,64,2048]{2,1,0:T(8,128)(2,1)S(1)} %get-tuple-element.43), kind=kOutput, calls=%fused_computation.52 | convolution fusion | flops 2148532224 | bytes 19398656 | tf_op jit(solution)/shard_map/schw,pkw->kpsch/dot_general | solution.py:35
  20.6 4.9 %fusion.31 = f32[64,2,1,32,128]{4,3,1,0,2:T(8,128)S(1)} fusion(f32[64,2,32,128]{3,0,2,1:T(8,128)} %fusion.37, f32[128,64]{1,0:T(8,128)S(1)} %get-tuple-element.39, f32[128,64]{1,0:T(8,128)S(1)} %get-tuple-element.38), kind=kOutput, calls=%fused_computation.50 | convolution fusion | flops 805322752 | bytes 4259840 | tf_op jit(solution)/shard_map/kpsch,hj->kpscj/dot_general | solution.py:43
  26.2 1.3 pad_maximum_fusion.3
  27.5 60.3 %reduce-scatter.3.cloned.1.call-done = f32[4,1,32,128]{3,2,0,1:T(8,128)} async-done(((f32[64,1,32,128]{3,2,0,1:T(8,128)}), f32[4,1,32,128]{3,2,0,1:T(8,128)}) %reduce-scatter.3.cloned.1.call-update) | async-done | bytes 65552 | tf_op jit(solution)/shard_map/reduce_scatter | solution.py:124
  87.8 1.0 slice_bitcast_fusion.37
  88.8 1.0 multiply_reduce_fusion.6
  90.0 2.9 fusion.66
  92.9 2.9 fusion.73
  95.8 3.5 fusion.25
  99.3 3.2 fusion.26
  102.6 0.6 constant_dynamic-update-slice_fusion.15
  103.3 0.6 constant_dynamic-update-slice_fusion.14
  103.9 0.6 constant_dynamic-update-slice_fusion.13
  104.6 0.6 constant_dynamic-update-slice_fusion.12
  105.2 0.6 constant_dynamic-update-slice_fusion.11
  105.9 0.6 constant_dynamic-update-slice_fusion.10
  106.5 0.6 constant_dynamic-update-slice_fusion.9
  107.2 0.6 constant_dynamic-update-slice_fusion.8
  107.8 0.6 constant_dynamic-update-slice_fusion.7
  108.5 0.6 constant_dynamic-update-slice_fusion.6
  109.1 0.6 constant_dynamic-update-slice_fusion.5
  109.8 0.6 constant_dynamic-update-slice_fusion.4
  110.4 0.6 constant_dynamic-update-slice_fusion.3
  111.1 0.6 constant_dynamic-update-slice_fusion.2
  111.7 0.6 constant_dynamic-update-slice_fusion.1
  112.3 0.6 constant_dynamic-update-slice_fusion
  113.0 4.3 all-to-all-start
  117.4 22.5 %fusion.17 = f32[128,2048,32]{1,2,0:T(8,128)} fusion(bf16[32,128,2048]{2,1,0:T(8,128)(2,1)} %bitcast.372, bf16[32,32]{1,0:T(8,128)(2,1)S(1)} %copy-done), kind=kOutput, calls=%fused_computation.21 | convolution fusion | flops 536870912 | bytes 50333696 | tf_op jit(solution)/shard_map/co,schw->sohw/dot_general | solution.py:142
  140.3 1.3 copy.70
  141.6 45.4 %convert_reduce_fusion = (f32[32]{0:T(128)S(1)}, bf16[1,32,128,2048]{3,2,1,0:T(8,128)(2,1)}) fusion(bf16[1,32,128,2048]{3,2,1,0:T(8,128)(2,1)} %param.6, f32[32]{0:T(128)S(1)} %copy-done.3, f32[128,2048,32]{1,2,0:T(8,128)} %fusion.17, bf16[1,64,2048]{2,1,0:T(8,128)(2,1)S(1)} %get-tuple-element.42, bf16[1,64,2048]{2,1,0:T(8,128)(2,1)S(1)} %get-tuple-element.43, ...), kind=kOutput, calls=%fused_computation.11 | convolution fusion | flops 2290352128 | bytes 68681984 | tf_op jit(solution)/shard_map/kpsch,pkw->schw/dot_general | solution.py:39
  187.0 11.0 %fusion.40 = f32[64,2,32,128]{3,0,2,1:T(8,128)} fusion(bf16[1,32,128,2048]{3,2,1,0:T(8,128)(2,1)} %get-tuple-element.41, bf16[1,64,2048]{2,1,0:T(8,128)(2,1)S(1)} %get-tuple-element.42, bf16[1,64,2048]{2,1,0:T(8,128)(2,1)S(1)} %get-tuple-element.43), kind=kOutput, calls=%fused_computation.53 | convolution fusion | flops 2148532224 | bytes 19398656 | tf_op jit(solution)/shard_map/schw,pkw->kpsch/dot_general | solution.py:35
  198.0 4.6 fusion.34
  203.2 1.3 pad_maximum_fusion.4
  204.5 78.0 %fusion.43 = f32[32,32]{0,1:T(8,128)S(1)} fusion(bf16[32,128,2048]{2,1,0:T(8,128)(2,1)} %bitcast.373, bf16[32,128,2048]{2,1,0:T(8,128)(2,1)} %bitcast.374), kind=kOutput, calls=%fused_computation.60 | convolution fusion | flops 536870912 | bytes 33558528 | tf_op jit(solution)/shard_map/schw,sohw->co/dot_general | solution.py:155
  282.6 62.9 %all-reduce = (f32[32,32]{0,1:T(8,128)S(1)}, f32[32]{0:T(128)S(1)}) all-reduce(f32[32,32]{0,1:T(8,128)S(1)} %fusion.43, f32[32]{0:T(128)S(1)} %get-tuple-element.40), channel_id=1, replica_groups=mesh['dom'=2,'space'=16] {'space'}, use_global_device_ids=true, to_apply=%region_2.3 | all-reduce | flops 1056 | bytes 8448 | tf_op jit(solution)/shard_map/psum | solution.py:157
  345.4 0.9 broadcast_multiply_fusion
  346.4 4.3 add_bitcast_fusion
  350.7 2.9 fusion.63
  353.7 2.9 fusion.70
  356.6 3.2 fusion.23
  359.8 3.2 fusion.24
  363.1 0.6 constant_dynamic-update-slice_fusion.31
  363.8 0.6 constant_dynamic-update-slice_fusion.30
  364.4 0.6 constant_dynamic-update-slice_fusion.29
  365.0 0.6 constant_dynamic-update-slice_fusion.28
  365.7 0.6 constant_dynamic-update-slice_fusion.27
  366.3 0.6 constant_dynamic-update-slice_fusion.26
  366.9 0.6 constant_dynamic-update-slice_fusion.25
  367.6 0.6 constant_dynamic-update-slice_fusion.24
  368.2 0.6 constant_dynamic-update-slice_fusion.23
  368.8 0.6 constant_dynamic-update-slice_fusion.22
  369.5 0.6 constant_dynamic-update-slice_fusion.21
  370.1 0.6 constant_dynamic-update-slice_fusion.20
  370.8 0.6 constant_dynamic-update-slice_fusion.19
  371.4 0.6 constant_dynamic-update-slice_fusion.18
  372.0 0.6 constant_dynamic-update-slice_fusion.17
  372.7 0.7 constant_dynamic-update-slice_fusion.16
  373.3 4.3 all-to-all-start.1
  377.7 0.7 copy.98
  378.9 35.8 %fusion.14 = f32[128,2048,32]{1,2,0:T(8,128)} fusion(bf16[32,128,2048]{2,1,0:T(8,128)(2,1)} %bitcast.375, bf16[32,32]{1,0:T(8,128)(2,1)S(1)} %copy-done), kind=kOutput, calls=%fused_computation.18 | convolution fusion | flops 536870912 | bytes 50333696 | tf_op jit(solution)/shard_map/co,sohw->schw/dot_general | solution.py:151
  414.7 3.6 pad_maximum_fusion
  418.3 1.3 copy.92
  419.6 33.6 %fusion.6 = bf16[1,32,128,2048]{3,2,1,0:T(8,128)(2,1)} fusion(f32[128,2048,32]{1,2,0:T(8,128)} %fusion.14, bf16[64,2,32,128]{3,2,1,0:T(8,128)(2,1)S(1)} %bitcast.376, bf16[1,64,2048]{2,1,0:T(8,128)(2,1)S(1)} %get-tuple-element.42, bf16[1,64,2048]{2,1,0:T(8,128)(2,1)S(1)} %get-tuple-element.43), kind=kOutput, calls=%fused_computation.8 | convolution fusion | flops 2164523008 | bytes 51904512 | tf_op jit(solution)/shard_map/kpsch,pkw->schw/dot_general | solution.py:39
  (30 shorter events, 3.0 us)
Async XLA Ops:
  7.2 110.2 %copy-start = (bf16[32,32]{1,0:T(8,128)(2,1)S(1)}, bf16[32,32]{1,0:T(8,128)(2,1)}, u32[]{:S(2)}) copy-start(bf16[32,32]{1,0:T(8,128)(2,1)} %param.8) | copy-start | bytes 6148
  7.2 80.6 %reduce-scatter.3.cloned.1.call-start = ((), (), s32[]{:S(2)}) async-start(), calls=%async_computation.4 | async-start | bytes 1114112 | tf_op jit(solution)/shard_map/reduce_scatter | solution.py:124
  9.8 79.0 %copy-start.1 = (f32[4,32,32,128]{3,2,1,0:T(8,128)S(1)}, f32[4,32,32,128]{3,2,1,0:T(8,128)}, u32[]{:S(2)}) copy-start(f32[4,32,32,128]{3,2,1,0:T(8,128)} %param.7) | copy-start | bytes 6291460
  113.0 27.3 %all-to-all-start = ((bf16[16,4,2,1,32,128]{5,4,1,2,3,0:T(8,128)(2,1)}), bf16[16,4,2,1,32,128]{5,4,1,2,3,0:T(8,128)(2,1)}, u32[]{:S(2)}, u32[]{:S(2)}) async-start(bf16[16,4,2,1,32,128]{5,4,1,2,3,0:T(8,128)(2,1)} %constant_dynamic-update-slice_fusion), calls=%async_computation.1 | async-start | bytes 2097152 | tf_op jit(solution)/shard_map/all_to_all | solution.py:132
  117.3 228.1 %reduce-scatter.5.cloned.1.call-start = ((), (), s32[]{:S(2)}) async-start(), calls=%async_computation.5 | async-start | bytes 1114112 | tf_op jit(solution)/shard_map/reduce_scatter | solution.py:124
  117.4 24.2 %copy-start.3 = (f32[32]{0:T(128)S(1)}, f32[32]{0:T(128)}, u32[]{:S(2)}) copy-start(f32[32]{0:T(128)} %param.9) | copy-start | bytes 388
  373.3 45.0 %all-to-all-start.1 = ((bf16[16,4,2,1,32,128]{5,4,1,2,3,0:T(8,128)(2,1)}), bf16[16,4,2,1,32,128]{5,4,1,2,3,0:T(8,128)(2,1)}, u32[]{:S(2)}, u32[]{:S(2)}) async-start(bf16[16,4,2,1,32,128]{5,4,1,2,3,0:T(8,128)(2,1)} %constant_dynamic-update-slice_fusion.16), calls=%async_computation.3 | async-start | bytes 2097152 | tf_op jit(solution)/shard_map/all_to_all | solution.py:132
  378.9 35.8 %copy-start.2 = (f32[4,32,32,64]{3,2,1,0:T(8,128)S(1)}, f32[4,32,32,64]{3,2,1,0:T(8,128)}, u32[]{:S(2)}) copy-start(f32[4,32,32,64]{3,2,1,0:T(8,128)} %get-tuple-element.28) | copy-start | bytes 3145732
Sparse Core Ops, SparseCore 0:
  27.6 60.1 reduce-scatter.2
  204.7 59.4 reduce-scatter.4
